TPU v7x, 32 devices: a whole 2x2x4 slice. The times are simulated.
32 devices in a mesh: seq: 8 (over z, x), ch: 4 (over y, core).
Axes of the slice: x: 2, y: 2, z: 4, core: 2. Of those that a mesh axis runs over, the one named last changes fastest.
Arguments:
- tokens: bfloat16 [2048, 8192], P('seq', 'ch'), may hold values from -6 to 6
- proj_weight: bfloat16 [3, 8192, 4096], P(None, None, 'ch'), may hold values from -0.0625 to 0.0625
- short_taps: float32 [3, 7, 4096], P(None, None, 'ch'), may hold values from -2.4 to 2.4
- long_filter: float32 [2048, 4096], P('seq', 'ch'), may hold values from -0.125 to 0.125
- skip_gain: float32 [4096], P('ch'), may hold values from 0.5 to 1.5
Outputs:
- operator_out: bfloat16 [2048, 4096], P('seq', 'ch')
All inputs are finite; a program needn't handle non-finite values.
Results may differ from a plain program's by a relative error of at most 0.0064.
Values may be sent and summed in bfloat16 or wider, within the bound.
A program may use at most 128 MiB of HBM per device.

v0:
```python
import math

import jax
import jax.numpy as jnp
from jax import lax
from jax.sharding import PartitionSpec as P

TAPS = 7


HIGH = lax.Precision.HIGHEST


def shifted(value, axis, by):
    size = lax.axis_size(axis)
    pairs = [(i, i + by) for i in range(size) if 0 <= i + by < size]
    return lax.ppermute(value, axis, pairs)


def spread_out(values):
    return lax.all_to_all(values, "seq", split_axis=2, concat_axis=1, tiled=True)


def collect_in(values):
    return lax.all_to_all(values, "seq", split_axis=1, concat_axis=2, tiled=True)


def angle_table(first, second, modulus):
    index_prod = first[:, None] * second[None, :] % modulus
    angles = index_prod.astype(jnp.float32) * (2.0 * math.pi / modulus)
    return (jnp.cos(angles), jnp.sin(angles))


def frequency_order(seq_count):
    places = jnp.arange(2 * seq_count, dtype=jnp.int32)
    owner = places // 2
    second = places % 2
    mirror = jnp.where(second == 0, owner, 2 * seq_count - owner)
    return jnp.where(owner == 0, second * seq_count, mirror)


def long_convolution(signal, kernel):
    row_count = signal.shape[0]
    seq_count = lax.axis_size("seq")
    slice_rows = row_count // seq_count
    seq_total = seq_count * row_count
    fft_length = 2 * seq_total
    seq_index = lax.axis_index("seq")
    stacked = jnp.stack([signal, kernel])[:, None]
    spread = spread_out(stacked)
    freq_outer = frequency_order(seq_count)
    time_outer = jnp.arange(seq_count, dtype=jnp.int32)
    cos_outer, sin_outer = angle_table(freq_outer, time_outer, 2 * seq_count)
    inner_pos = seq_index * slice_rows + jnp.arange(slice_rows, dtype=jnp.int32)
    cos_twist, sin_twist = angle_table(freq_outer, inner_pos, fft_length)
    inner_index = jnp.arange(row_count, dtype=jnp.int32)
    cos_inner, sin_inner = angle_table(inner_index, inner_index, row_count)
    real_part = jnp.einsum("ft,atjc->afjc", cos_outer, spread, precision=HIGH)
    imag_part = -jnp.einsum("ft,atjc->afjc", sin_outer, spread, precision=HIGH)
    twist_cos = cos_twist[None, :, :, None]
    twist_sin = sin_twist[None, :, :, None]
    twisted_real = real_part * twist_cos + imag_part * twist_sin
    twisted_imag = imag_part * twist_cos - real_part * twist_sin
    paired = collect_in(jnp.concatenate([twisted_real, twisted_imag], 0))
    paired_real = paired[:2]
    paired_imag = paired[2:]
    freq_real = jnp.einsum("gt,aptc->apgc", cos_inner, paired_real, precision=HIGH) + jnp.einsum(
        "gt,aptc->apgc", sin_inner, paired_imag, precision=HIGH
    )
    freq_imag = jnp.einsum("gt,aptc->apgc", cos_inner, paired_imag, precision=HIGH) - jnp.einsum(
        "gt,aptc->apgc", sin_inner, paired_real, precision=HIGH
    )
    prod_real = freq_real[0] * freq_real[1] - freq_imag[0] * freq_imag[1]
    prod_imag = freq_real[0] * freq_imag[1] + freq_imag[0] * freq_real[1]
    final_factor = 1.0 / fft_length
    back_real = jnp.einsum("tg,pgc->ptc", cos_inner, prod_real, precision=HIGH) - jnp.einsum(
        "tg,pgc->ptc", sin_inner, prod_imag, precision=HIGH
    )
    back_imag = jnp.einsum("tg,pgc->ptc", cos_inner, prod_imag, precision=HIGH) + jnp.einsum(
        "tg,pgc->ptc", sin_inner, prod_real, precision=HIGH
    )
    returned = spread_out(jnp.stack([back_real, back_imag]))
    back_cos = cos_twist[:, :, None]
    back_sin = sin_twist[:, :, None]
    untwist_real = returned[0] * back_cos - returned[1] * back_sin
    untwist_imag = returned[0] * back_sin + returned[1] * back_cos
    time_values = jnp.einsum("ft,fjc->tjc", cos_outer, untwist_real, precision=HIGH) - jnp.einsum(
        "ft,fjc->tjc", sin_outer, untwist_imag, precision=HIGH
    )
    time_values = time_values * final_factor
    gathered = collect_in(time_values[None])
    return gathered[0, 0]


def per_device(tokens, proj_weight, short_taps, long_filter, skip_gain):
    row_count = tokens.shape[0]
    chan_count = proj_weight.shape[2]
    projected = jnp.einsum(
        "td,jdc->jtc",
        lax.all_gather(tokens, "ch", axis=1, tiled=True),
        proj_weight,
        preferred_element_type=jnp.float32,
    ).astype(jnp.bfloat16)
    rim_rows = shifted(projected[:, row_count - (TAPS - 1) :], "seq", 1)
    extended = jnp.concatenate([rim_rows, projected], 1)
    filtered = jnp.zeros((3, row_count, chan_count), jnp.float32)
    for tap_index in range(TAPS):
        begin = TAPS - 1 - tap_index
        filtered = filtered + short_taps[:, tap_index][:, None, :] * extended[
            :, begin : begin + row_count
        ].astype(jnp.float32)
    query_part = filtered[0]
    gated_input = filtered[1] * filtered[2]
    long_conv = long_convolution(gated_input, long_filter)
    return (query_part * (long_conv + skip_gain * gated_input)).astype(jnp.bfloat16)


def solution(mesh):
    return jax.shard_map(
        per_device,
        mesh=mesh,
        in_specs=(
            P("seq", "ch"),
            P(None, None, "ch"),
            P(None, None, "ch"),
            P("seq", "ch"),
            P("ch"),
        ),
        out_specs=P("seq", "ch"),
        check_vma=False,
    )
```

profile of v0, /device:TPU:0, one launch (start us, length us, event | category | flops | bytes accessed | tf_op | source)
XLA Modules:
  0.0 549.7 jit_solution(15885342616061010418)
XLA Ops:
  6.5 0.0 all-gather.2.cloned.1.call-start
  6.5 0.7 all-gather.2.cloned.1.call-update
  7.3 1.3 fusion.146
  8.6 37.5 %all-gather.2.cloned.1.call-done = bf16[256,8192]{1,0:T(8,128)(2,1)} async-done(((bf16[256,2048]{1,0:T(8,128)(2,1)}), bf16[256,8192]{1,0:T(8,128)(2,1)}) %all-gather.2.cloned.1.call-update) | async-done | bytes 4194320 | tf_op jit(solution)/shard_map/all_gather | solution.py:100
  46.1 21.8 %fusion.34 = bf16[3,256,1024]{2,1,0:T(8,128)(2,1)S(1)} fusion(bf16[3,8192,1024]{2,1,0:T(8,128)(2,1)} %param.6, bf16[256,8192]{1,0:T(8,128)(2,1)} %all-gather.2.cloned.1.call-done), kind=kOutput, calls=%fused_computation.55 | convolution fusion | flops 12885688320 | bytes 56098816 | tf_op jit(solution)/shard_map/td,jdc->jtc/dot_general | solution.py:98
  68.0 3.4 collective-permute-start
  71.4 1.7 collective-permute-done
  73.1 0.0 copy-start
  73.1 2.9 multiply_add_fusion
  76.0 0.1 slice_multiply_fusion
  76.1 0.0 copy-done
  76.1 0.2 maximum_bitcast_fusion
  76.3 2.9 copy.73
  79.2 7.0 %all-to-all-start = ((f32[2,1,256,1024]{3,0,1,2:T(2,128)}), f32[2,1,256,1024]{3,0,1,2:T(2,128)}, u32[]{:S(2)}, u32[]{:S(2)}) async-start(f32[2,1,256,1024]{3,0,1,2:T(2,128)} %copy.73), calls=%async_computation | async-start | bytes 4194304 | tf_op jit(solution)/shard_map/all_to_all | solution.py:21
  86.2 0.1 fusion.86
  86.4 0.1 copy.76
  86.5 0.1 copy.78
  86.5 47.2 %all-to-all-done = f32[2,1,256,1024]{3,0,1,2:T(2,128)} async-done(((f32[2,1,256,1024]{3,0,1,2:T(2,128)}), f32[2,1,256,1024]{3,0,1,2:T(2,128)}, u32[]{:S(2)}, u32[]{:S(2)}) %all-to-all-start) | async-done | bytes 2097184 | tf_op jit(solution)/shard_map/all_to_all | solution.py:21
  133.8 2.3 copy.74
  136.0 6.1 %fusion.18 = f32[2,32,1024,16]{2,3,1,0:T(8,128)S(1)} fusion(f32[2,8,32,1024]{3,2,1,0:T(8,128)S(1)} %bitcast.158, s32[16]{0:T(128)S(1)} %compare_select_fusion.1), kind=kOutput, calls=%fused_computation.41 | convolution fusion | flops 100665088 | bytes 6291520 | tf_op jit(solution)/shard_map/ft,atjc->afjc/dot_general | solution.py:59
  142.2 7.9 %fusion = (f32[2,16,32,1024]{3,1,2,0:T(8,128)}, f32[2,16,32,1024]{3,1,2,0:T(8,128)}) fusion(f32[2,32,1024,16]{2,3,1,0:T(8,128)S(1)} %fusion.18, f32[16,32]{0,1:T(8,128)S(1)} %copy.78, f32[16,32]{0,1:T(8,128)S(1)} %copy.76, s32[16]{0:T(128)S(1)} %compare_select_fusion.1, f32[2,8,32,1024]{3,2,1,0:T(8,128)S(1)} %bitcast.159), kind=kOutput, calls=%fused_computation.4 | convolution fusion | flops 108005120 | bytes 14684224 | tf_op jit(solution)/shard_map/ft,atjc->afjc/dot_general | solution.py:58
  150.1 4.3 pad_maximum_fusion
  154.4 8.1 %copy.79 = f32[4,16,32,1024]{3,2,0,1:T(8,128)} copy(f32[4,16,32,1024]{3,1,2,0:T(8,128)S(1)} %pad_maximum_fusion) | data formatting | bytes 16777216 | tf_op jit(solution)/shard_map/concatenate | solution.py:64
  162.5 186.9 %all_to_all.51 = f32[4,16,32,1024]{3,2,0,1:T(8,128)S(1)} all-to-all(f32[4,16,32,1024]{3,2,0,1:T(8,128)} %copy.79), channel_id=1, replica_groups=mesh['seq'=8,'ch'=4] {'seq'}, dimensions={1} | all-to-all | bytes 16777216 | tf_op jit(solution)/shard_map/all_to_all | solution.py:25
  349.4 1.7 copy.80
  351.1 1.7 fusion.144
  352.7 0.5 copy.81
  353.3 7.5 %fusion.60 = f32[2,2,1024,256]{3,2,1,0:T(8,128)S(1)} fusion(f32[2,2,256,1024]{3,2,1,0:T(8,128)S(1)} %bitcast.153), kind=kOutput, calls=%fused_computation.79 | convolution fusion | flops 3222142976 | bytes 8388608 | tf_op jit(solution)/shard_map/gt,aptc->apgc/dot_general | solution.py:67
  360.8 0.5 copy.83
  361.3 7.9 %fusion.58 = f32[2,2,1024,256]{3,2,1,0:T(8,128)S(1)} fusion(f32[2,2,256,1024]{3,2,1,0:T(8,128)S(1)} %bitcast.155), kind=kOutput, calls=%fused_computation.77 | convolution fusion | flops 3222142976 | bytes 8388608 | tf_op jit(solution)/shard_map/gt,aptc->apgc/dot_general | solution.py:70
  369.3 7.7 %add_bitcast_fusion = f32[2,2,256,1024]{2,3,1,0:T(8,128)S(1)} fusion(f32[2,2,1024,256]{3,2,1,0:T(8,128)S(1)} %fusion.60, f32[2,2,256,1024]{3,2,1,0:T(8,128)S(1)} %bitcast.156), kind=kOutput, calls=%fused_computation.11 | convolution fusion | flops 3223191552 | bytes 12582912 | tf_op jit(solution)/shard_map/gt,aptc->apgc/dot_general | solution.py:67
  377.0 7.5 %subtract_bitcast_fusion = f32[2,2,256,1024]{2,3,1,0:T(8,128)S(1)} fusion(f32[2,2,1024,256]{3,2,1,0:T(8,128)S(1)} %fusion.58, f32[2,2,256,1024]{3,2,1,0:T(8,128)S(1)} %bitcast.154), kind=kOutput, calls=%fused_computation.10 | convolution fusion | flops 3223191552 | bytes 12582912 | tf_op jit(solution)/shard_map/gt,aptc->apgc/dot_general | solution.py:70
  384.6 0.6 multiply_subtract_fusion
  385.2 3.1 fusion.6
  388.3 2.8 fusion.8
  391.1 2.9 subtract_bitcast_fusion.1
  394.0 2.9 add_bitcast_fusion.1
  396.9 2.2 pad_maximum_fusion.1
  399.1 7.4 %copy.87 = f32[2,2,256,1024]{3,1,0,2:T(2,128)} copy(f32[2,2,256,1024]{2,3,1,0:T(8,128)} %pad_maximum_fusion.1) | data formatting | bytes 8388608 | tf_op jit(solution)/shard_map/stack | solution.py:82
  406.5 96.9 %all_to_all.52 = f32[2,2,256,1024]{3,1,0,2:T(2,128)S(1)} all-to-all(f32[2,2,256,1024]{3,1,0,2:T(2,128)} %copy.87), channel_id=1, replica_groups=mesh['seq'=8,'ch'=4] {'seq'}, dimensions={2} | all-to-all | bytes 8388608 | tf_op jit(solution)/shard_map/all_to_all | solution.py:21
  503.4 2.4 copy.88
  505.9 0.6 fusion.145
  506.4 0.2 copy.89
  506.7 0.2 copy.90
  506.9 0.5 fusion.4
  507.5 2.2 fusion.14
  509.7 2.3 fusion.43
  512.0 0.0 copy-start.1
  512.0 0.6 copy.93
  512.6 28.5 %all_to_all.53 = f32[1,8,32,1024]{3,2,0,1:T(8,128)S(1)} all-to-all(f32[1,8,32,1024]{3,2,0,1:T(8,128)S(1)} %copy.93), channel_id=1, replica_groups=mesh['seq'=8,'ch'=4] {'seq'}, dimensions={1} | all-to-all | bytes 2097152 | tf_op jit(solution)/shard_map/all_to_all | solution.py:25
  541.1 0.0 copy-done.1
  541.1 1.2 fusion.47
  (7 shorter events, 0.1 us)
Async XLA Ops:
  6.5 39.6 %all-gather.2.cloned.1.call-start = ((), (), s32[]{:S(2)}) async-start(), calls=%async_computation.4 | async-start | bytes 5242880 | tf_op jit(solution)/shard_map/all_gather | solution.py:100
  68.0 5.1 collective-permute-start
  73.1 3.0 copy-start
  79.2 54.5 %all-to-all-start = ((f32[2,1,256,1024]{3,0,1,2:T(2,128)}), f32[2,1,256,1024]{3,0,1,2:T(2,128)}, u32[]{:S(2)}, u32[]{:S(2)}) async-start(f32[2,1,256,1024]{3,0,1,2:T(2,128)} %copy.73), calls=%async_computation | async-start | bytes 4194304 | tf_op jit(solution)/shard_map/all_to_all | solution.py:21
  512.0 29.1 %copy-start.1 = (f32[1024]{0:T(1024)S(1)}, f32[1024]{0:T(1024)}, u32[]{:S(2)}) copy-start(f32[1024]{0:T(1024)} %param.9) | copy-start | bytes 12292
Sparse Core Ops, SparseCore 0:
  8.9 37.1 all-gather.1
where the time goes:
time: 555 us; the launch traced here: 550 us
  blocking collectives  312 us (56%)
  waiting for transfers between devices  87.2 us (16%)
  matrix products  82.8 us (15%)
  local copies, waits for them, and re-layouts  30.7 us (6%)
  between operations  14.1 us (3%)
  other arithmetic  12.3 us (2%)
  starting transfers between devices  10.3 us (2%)
    all_to_all x2, blocking collectives, collect_in(): lax.all_to_all(values, 'seq', split_axis=1, concat_axis=2, tiled=True)  215 us
    all_to_all x1, blocking collectives, spread_out(): lax.all_to_all(values, 'seq', split_axis=2, concat_axis=1, tiled=True)  96.9 us
    all_to_all x1, waiting for transfers between devices, spread_out(): lax.all_to_all(values, 'seq', split_axis=2, concat_axis=1, tiled=True)  47.2 us
    all_gather x1, waiting for transfers between devices, per_device(): lax.all_gather(tokens, 'ch', axis=1, tiled=True)  37.5 us
    dot_general x1, matrix products, per_device(): jnp.einsum('td,jdc->jtc', lax.all_gather(tokens, 'ch', axis=1, tiled=True...  21.8 us
  transfers between devices with their start and end apart: 3, of which 3 were waited for; matrix products, arithmetic and copies ran while one was open for 0% of the time, Pallas kernels for 0%

commit v1 on v0

--- a/solution.py
+++ b/solution.py
@@ -1,11 +1,16 @@
+import functools
 import math
 
 import jax
 import jax.numpy as jnp
+import numpy as np
 from jax import lax
+from jax.experimental import pallas as pl
+from jax.experimental.pallas import tpu as pltpu
 from jax.sharding import PartitionSpec as P
 
 TAPS = 7
+LANES = 128
 
 
 HIGH = lax.Precision.HIGHEST
@@ -39,7 +44,7 @@
     return jnp.where(owner == 0, second * seq_count, mirror)
 
 
-def long_convolution(signal, kernel):
+def spread_convolution(signal, kernel):
     row_count = signal.shape[0]
     seq_count = lax.axis_size("seq")
     slice_rows = row_count // seq_count
@@ -92,9 +97,155 @@
     return gathered[0, 0]
 
 
+def transform_tables(blocks, rows):
+    index = np.arange(rows)
+    angle = 2.0 * np.pi * (index[:, None] * index[None, :] % rows) / rows
+    cos, sin = np.cos(angle), np.sin(angle)
+    there = np.block([[cos, sin], [-sin, cos]])
+    back = np.block([[cos, -sin], [sin, cos]])
+    twist = 2.0 * np.pi * np.arange(blocks + 1)[:, None] * index[None, :] / (2 * blocks * rows)
+    twist = np.stack([np.cos(twist), np.sin(twist)], 1)[..., None]
+    twist = np.broadcast_to(twist, twist.shape[:3] + (LANES,))
+    return (
+        jnp.asarray(there, jnp.bfloat16),
+        jnp.asarray(back, jnp.bfloat16),
+        jnp.asarray(twist, jnp.float32),
+    )
+
+
+def weighted(terms):
+    total = None
+    for factor, array in terms:
+        if abs(factor) < 1e-12:
+            continue
+        if abs(factor - 1.0) < 1e-12:
+            total = array if total is None else total + array
+        elif abs(factor + 1.0) < 1e-12:
+            total = -array if total is None else total - array
+        else:
+            total = factor * array if total is None else total + factor * array
+    return total
+
+
+def fold(load, blocks):
+    half = blocks // 2
+    first, middle = load(0), load(half)
+    sums, gaps = [], []
+    for j in range(1, half):
+        low, high = load(j), load(blocks - j)
+        sums.append(low + high)
+        gaps.append(low - high)
+    return first, middle, sums, gaps
+
+
+def outer_stage(folded, freq, blocks):
+    first, middle, sums, gaps = folded
+    half = blocks // 2
+    even = freq % 2 == 0
+    cos_of = lambda j: math.cos(math.pi * freq * j / blocks)
+    sin_of = lambda j: math.sin(math.pi * freq * j / blocks)
+    with_cos, with_sin = (sums, gaps) if even else (gaps, sums)
+    real = weighted(
+        [(1.0, first), (cos_of(half), middle)] + [(cos_of(j), with_cos[j - 1]) for j in range(1, half)]
+    )
+    imag = weighted([(-sin_of(half), middle)] + [(-sin_of(j), with_sin[j - 1]) for j in range(1, half)])
+    return real, imag
+
+
+def twisted_stage(folded, freq, blocks, cos, sin):
+    real, imag = outer_stage(folded, freq, blocks)
+    if imag is None:
+        return jnp.concatenate([real * cos, -(real * sin)], 0).astype(jnp.bfloat16)
+    return jnp.concatenate([real * cos + imag * sin, imag * cos - real * sin], 0).astype(jnp.bfloat16)
+
+
+def local_convolution(blocks, rows, load_signal, load_filter, there, back, twist):
+    half = blocks // 2
+    signal, filt = fold(load_signal, blocks), fold(load_filter, blocks)
+    cos_even, sin_even = [None] * (half + 1), [None] * (half + 1)
+    cos_odd, sin_odd = [None] * (half + 1), [None] * (half + 1)
+    plus = lambda old, new: new if old is None else (old if new is None else old + new)
+    for freq in range(blocks + 1):
+        cos, sin = twist[freq, 0], twist[freq, 1]
+        stacked = jnp.concatenate(
+            [
+                twisted_stage(signal, freq, blocks, cos, sin),
+                twisted_stage(filt, freq, blocks, cos, sin),
+            ],
+            1,
+        )
+        spectrum = jnp.dot(there[...], stacked, preferred_element_type=jnp.float32)
+        sig_real, sig_imag = spectrum[:rows, :LANES], spectrum[rows:, :LANES]
+        fil_real, fil_imag = spectrum[:rows, LANES:], spectrum[rows:, LANES:]
+        scale = (1.0 if freq in (0, blocks) else 2.0) / (2 * blocks * rows)
+        product = jnp.concatenate(
+            [
+                (sig_real * fil_real - sig_imag * fil_imag) * scale,
+                (sig_real * fil_imag + sig_imag * fil_real) * scale,
+            ],
+            0,
+        ).astype(jnp.bfloat16)
+        values = jnp.dot(back[...], product, preferred_element_type=jnp.float32)
+        real, imag = values[:rows], values[rows:]
+        out_real, out_imag = real * cos - imag * sin, real * sin + imag * cos
+        cos_sum, sin_sum = (cos_even, sin_even) if freq % 2 == 0 else (cos_odd, sin_odd)
+        for j in range(half + 1):
+            angle = math.pi * freq * j / blocks
+            cos_sum[j] = plus(cos_sum[j], weighted([(math.cos(angle), out_real)]))
+            sin_sum[j] = plus(sin_sum[j], weighted([(math.sin(angle), out_imag)]))
+    minus = lambda left, right: left if right is None else (-right if left is None else left - right)
+    result = [None] * blocks
+    for j in range(half + 1):
+        result[j] = minus(plus(cos_even[j], cos_odd[j]), plus(sin_even[j], sin_odd[j]))
+        if 0 < j < half:
+            result[blocks - j] = plus(minus(cos_even[j], cos_odd[j]), minus(sin_even[j], sin_odd[j]))
+    return result
+
+
+def convolution_kernel(blocks, rows, signal, filt, there, back, twist, out):
+    result = local_convolution(
+        blocks,
+        rows,
+        lambda j: signal[j].astype(jnp.float32),
+        lambda j: filt[j].astype(jnp.float32),
+        there,
+        back,
+        twist,
+    )
+    for j in range(blocks):
+        out[j] = result[j].astype(out.dtype)
+
+
+def narrow_convolution(signal, spread_filter):
+    blocks = lax.axis_size("seq")
+    rows = signal.shape[0]
+    spread_signal = exchange(signal)
+    there, back, twist = transform_tables(blocks, rows)
+    out = pl.pallas_call(
+        functools.partial(convolution_kernel, blocks, rows),
+        out_shape=jax.ShapeDtypeStruct((blocks, rows, LANES), jnp.bfloat16),
+        in_specs=[pl.BlockSpec(memory_space=pltpu.VMEM)] * 5,
+        out_specs=pl.BlockSpec(memory_space=pltpu.VMEM),
+        compiler_params=pltpu.CompilerParams(vmem_limit_bytes=48 * 1024 * 1024),
+        name="long_convolution",
+    )(spread_signal, spread_filter, there, back, twist)
+    gathered = lax.all_to_all(out, "seq", split_axis=0, concat_axis=0, tiled=True)
+    return jnp.swapaxes(gathered, 0, 1).reshape(signal.shape).astype(jnp.float32)
+
+
+def exchange(values):
+    blocks = lax.axis_size("seq")
+    parts = values.astype(jnp.bfloat16).reshape(values.shape[0], blocks, LANES)
+    return lax.all_to_all(jnp.swapaxes(parts, 0, 1), "seq", split_axis=0, concat_axis=0, tiled=True)
+
+
 def per_device(tokens, proj_weight, short_taps, long_filter, skip_gain):
     row_count = tokens.shape[0]
     chan_count = proj_weight.shape[2]
+    seq_count = lax.axis_size("seq")
+    narrow = chan_count == seq_count * LANES and row_count % 16 == 0 and seq_count % 4 == 0
+    if narrow:
+        spread_filter = exchange(long_filter)
     projected = jnp.einsum(
         "td,jdc->jtc",
         lax.all_gather(tokens, "ch", axis=1, tiled=True),
@@ -111,7 +262,10 @@
         ].astype(jnp.float32)
     query_part = filtered[0]
     gated_input = filtered[1] * filtered[2]
-    long_conv = long_convolution(gated_input, long_filter)
+    if narrow:
+        long_conv = narrow_convolution(gated_input, spread_filter)
+    else:
+        long_conv = spread_convolution(gated_input, long_filter)
     return (query_part * (long_conv + skip_gain * gated_input)).astype(jnp.bfloat16)
 
 

time: 555 us -> 141 us (0.25)
  blocking collectives: 312 us -> 37.6 us
  matrix products: 82.8 us -> 21.8 us
  waiting for transfers between devices: 87.2 us -> 31.5 us
  local copies, waits for them, and re-layouts: 30.7 us -> 14.9 us
    all_to_all x3 -> x2, blocking collectives: 312 us -> 37.6 us  [the longest x1 20.1 us: exchange(): lax.all_to_all(jnp.swapaxes(parts, 0, 1), 'seq', split_axis=0, concat_axi...]
    dot_general x12 -> x0, matrix products: 61 us -> none  [the longest x1 7.94 us: long_convolution(): real_part = jnp.einsum('ft,atjc->afjc', cos_outer, spread, precision=HIGH)]
    all_to_all x1, waiting for transfers between devices: 47.2 us -> 0.01 us  [exchange(): lax.all_to_all(jnp.swapaxes(parts, 0, 1), 'seq', split_axis=0, concat_axi...]
    convert_element_type x0 -> x4, local copies, waits for them, and re-layouts: none -> 9.6 us  [the longest x2 5.4 us: narrow_convolution(): jnp.swapaxes(gathered, 0, 1).reshape(signal.shape).astype(jnp.float32)]
    all_gather x1, waiting for transfers between devices: 37.5 us -> 29.1 us  [per_device(): lax.all_gather(tokens, 'ch', axis=1, tiled=True)]
    concatenate x1 -> x0, local copies, waits for them, and re-layouts: 8.08 us -> none  [long_convolution(): paired = collect_in(jnp.concatenate([twisted_real, twisted_imag], 0))]
    another operation x1 -> x0, local copies, waits for them, and re-layouts: 7.42 us -> none  [long_convolution(): returned = spread_out(jnp.stack([back_real, back_imag]))]
    all_to_all x3 -> x0, local copies, waits for them, and re-layouts: 6.35 us -> none  [the longest x2 4.7 us: spread_out(): lax.all_to_all(values, 'seq', split_axis=2, concat_axis=1, tiled=True)]
  transfers between devices with their start and end apart: 3 -> 3, of which waited for: 3 -> 2; matrix products, arithmetic and copies ran while one was open for 0% -> 23% of each run, Pallas kernels for 0% -> 0%
where the time goes in v1:
time: 141 us
  blocking collectives  37.6 us (27%)
  waiting for transfers between devices  31.5 us (22%)
  matrix products  21.8 us (15%)
  local copies, waits for them, and re-layouts  14.9 us (11%)
  between operations  13.5 us (10%)
  starting transfers between devices  10.6 us (8%)
  other arithmetic  7.3 us (5%)
  Pallas kernels  3.76 us (3%)
    all_gather x1, waiting for transfers between devices, per_device(): lax.all_gather(tokens, 'ch', axis=1, tiled=True)  29.1 us
    dot_general x1, matrix products, per_device(): jnp.einsum('td,jdc->jtc', lax.all_gather(tokens, 'ch', axis=1, tiled=True...  21.8 us
    all_to_all x1, blocking collectives, exchange(): lax.all_to_all(jnp.swapaxes(parts, 0, 1), 'seq', split_axis=0, concat_axi...  20.1 us
    all_to_all x1, blocking collectives, narrow_convolution(): lax.all_to_all(out, 'seq', split_axis=0, concat_axis=0, tiled=True)  17.4 us
    all_to_all x1, starting transfers between devices, exchange(): lax.all_to_all(jnp.swapaxes(parts, 0, 1), 'seq', split_axis=0, concat_axi...  7.25 us
    convert_element_type x2, local copies, waits for them, and re-layouts, narrow_convolution(): jnp.swapaxes(gathered, 0, 1).reshape(signal.shape).astype(jnp.float32)  5.4 us
    convert_element_type x2, local copies, waits for them, and re-layouts, exchange(): parts = values.astype(jnp.bfloat16).reshape(values.shape[0], blocks, LANES)  4.2 us
    unnamed x19, local copies, waits for them, and re-layouts  4.17 us
  transfers between devices with their start and end apart: 3, of which 2 were waited for; matrix products, arithmetic and copies ran while one was open for 23% of the time, Pallas kernels for 0%

profile of v1, /device:TPU:0, one launch (start us, length us, event | category | flops | bytes accessed | tf_op | source)
XLA Modules:
  0.0 140.9 jit_solution(16500441984884025623)
XLA Ops:
  6.5 0.0 copy-start.5
  6.5 0.0 all-gather.2.cloned.1.call-start
  6.5 0.7 all-gather.2.cloned.1.call-update
  7.3 1.4 %copy.11 = bf16[256,1024]{0,1:T(8,128)(2,1)S(1)} copy(f32[256,1024]{1,0:T(8,128)} %param.11) | data formatting | bytes 1572864 | tf_op args[3]
  8.7 1.0 copy.12
  9.7 7.3 %all-to-all-start.1 = ((bf16[8,256,128]{2,1,0:T(8,128)(2,1)}), bf16[8,256,128]{2,1,0:T(8,128)(2,1)S(1)}, u32[]{:S(2)}, u32[]{:S(2)}) async-start(bf16[8,256,128]{2,1,0:T(8,128)(2,1)} %bitcast.6), calls=%async_computation.1 | async-start | bytes 1048576 | tf_op jit(solution)/shard_map/all_to_all | solution.py:239
  17.0 0.0 copy-done.5
  17.0 0.1 fusion.17
  17.1 29.1 %all-gather.2.cloned.1.call-done = bf16[256,8192]{1,0:T(8,128)(2,1)} async-done(((bf16[256,2048]{1,0:T(8,128)(2,1)}), bf16[256,8192]{1,0:T(8,128)(2,1)}) %all-gather.2.cloned.1.call-update) | async-done | bytes 4194320 | tf_op jit(solution)/shard_map/all_gather | solution.py:251
  46.1 21.8 %fusion.10 = bf16[3,256,1024]{2,1,0:T(8,128)(2,1)S(1)} fusion(bf16[3,8192,1024]{2,1,0:T(8,128)(2,1)} %param.9, bf16[256,8192]{1,0:T(8,128)(2,1)} %all-gather.2.cloned.1.call-done), kind=kOutput, calls=%fused_computation.18 | convolution fusion | flops 12885688320 | bytes 56098816 | tf_op jit(solution)/shard_map/td,jdc->jtc/dot_general | solution.py:249
  68.0 3.4 %collective-permute-start = (bf16[3,6,1024]{2,1,0:T(8,128)(2,1)S(1)}, bf16[3,6,1024]{2,1,0:T(8,128)(2,1)S(1)}, u32[]{:S(2)}, u32[]{:S(2)}) collective-permute-start(bf16[3,6,1024]{2,1,0:T(8,128)(2,1)S(1)} %slice.68), channel_id=1, source_target_pairs={{0,4},{4,8},{8,12},{12,16},{16,20},{20,24},{24,28},{1,5},{5,9},{9,... | collective-permute-start | bytes 110600 | tf_op jit(solution)/shard_map/ppermute | solution.py:22
  71.4 1.7 %collective-permute-done = bf16[3,6,1024]{2,1,0:T(8,128)(2,1)S(1)} collective-permute-done((bf16[3,6,1024]{2,1,0:T(8,128)(2,1)S(1)}, bf16[3,6,1024]{2,1,0:T(8,128)(2,1)S(1)}, u32[]{:S(2)}, u32[]{:S(2)}) %collective-permute-start) | collective-permute-done | bytes 36896 | tf_op jit(solution)/shard_map/ppermute | solution.py:22
  73.1 2.9 %multiply_add_fusion = f32[3,256,1024]{2,1,0:T(8,128)S(1)} fusion(bf16[3,256,1024]{2,1,0:T(8,128)(2,1)S(1)} %fusion.10, bf16[3,6,1024]{2,1,0:T(8,128)(2,1)S(1)} %collective-permute-done, f32[3,1024]{1,0:T(4,128)S(1)} %get-tuple-element.12, f32[3,1024]{1,0:T(4,128)S(1)} %get-tuple-element.13, f32[3,1024]{1,0:T(4,128)S(1)} %get-tuple-element.14, ...), kind=kLoop, calls=%fused_computation.7 | loop fusion | flops 29884416 | bytes 4841472 | tf_op jit(solution)/shard_map/add | solution.py:260
  76.0 0.0 copy-start.3
  76.0 1.6 %copy-done.3 = f32[3,256,1024]{2,1,0:T(8,128)} copy-done((f32[3,256,1024]{2,1,0:T(8,128)}, f32[3,256,1024]{2,1,0:T(8,128)S(1)}, u32[]{:S(2)}) %copy-start.3) | copy-done | bytes 3145752
  77.6 0.0 copy-start
  77.6 0.0 copy-start.1
  77.6 0.9 fusion.16
  78.6 2.2 %copy.9 = bf16[1,256,1024]{1,2,0:T(8,128)(2,1)} copy(bf16[1,256,1024]{2,1,0:T(8,128)(2,1)} %fusion.16) | data formatting | bytes 1048576 | tf_op jit(solution)/shard_map/convert_element_type | solution.py:238
  80.7 2.0 %copy.10 = bf16[256,8,128]{2,0,1:T(8,128)(2,1)} copy(bf16[256,8,128]{0,2,1:T(8,128)(2,1)} %bitcast.47) | data formatting | bytes 1048576 | tf_op jit(solution)/shard_map/convert_element_type | solution.py:238
  82.8 0.0 all-to-all-done.1.filt
  82.8 20.1 %all_to_all.15.signal = bf16[8,256,128]{2,1,0:T(8,128)(2,1)S(1)} all-to-all(bf16[8,256,128]{2,1,0:T(8,128)(2,1)} %bitcast.46), channel_id=1, replica_groups=mesh['seq'=8,'ch'=4] {'seq'}, dimensions={0} | all-to-all | bytes 1048576 | tf_op jit(solution)/shard_map/all_to_all | solution.py:239
  102.9 0.0 copy-done
  102.9 0.0 copy-done.1
  102.9 0.0 copy-start.2
  102.9 1.0 copy-done.2
  103.9 3.8 %long_convolution.1 = bf16[8,256,128]{2,1,0:T(8,128)(2,1)S(1)} custom-call(bf16[8,256,128]{2,1,0:T(8,128)(2,1)S(1)} %all_to_all.15.signal, bf16[8,256,128]{2,1,0:T(8,128)(2,1)S(1)} %all-to-all-done.1.filt, bf16[512,512]{1,0:T(8,128)(2,1)S(1)} %copy-done.2, bf16[512,512]{1,0:T(8,128)(2,1)S(1)} %copy-done.1, f32[9,2,256,128]{3,2,1,0:T(8,128)S(1)} %copy-done), custom_call_target="tpu_custom_call" | custom-call | tf_op jit(solution)/shard_map/long_convolution/pallas_call | solution.py:224
  107.7 17.4 %all_to_all.16 = bf16[8,256,128]{2,1,0:T(8,128)(2,1)S(1)} all-to-all(bf16[8,256,128]{2,1,0:T(8,128)(2,1)S(1)} %long_convolution.1), channel_id=1, replica_groups=mesh['seq'=8,'ch'=4] {'seq'}, dimensions={0} | all-to-all | bytes 1048576 | tf_op jit(solution)/shard_map/all_to_all | solution.py:232
  125.1 0.0 copy-start.4
  125.1 0.0 copy-start.6
  125.1 1.1 convert_bitcast_fusion
  126.2 2.9 %copy.13 = f32[256,8,128]{0,2,1:T(8,128)} copy(f32[256,8,128]{2,0,1:T(8,128)} %convert_bitcast_fusion) | data formatting | bytes 2097152 | tf_op jit(solution)/shard_map/convert_element_type | solution.py:233
  129.1 2.5 %copy.14 = f32[256,1024]{1,0:T(8,128)} copy(f32[256,1024]{0,1:T(8,128)} %bitcast.44) | data formatting | bytes 2097152 | tf_op jit(solution)/shard_map/convert_element_type | solution.py:233
  131.6 0.0 copy-done.4
  131.6 0.0 copy-done.6
  131.6 2.4 %fusion.14 = bf16[256,1024]{1,0:T(8,128)(2,1)} fusion(f32[3,256,1024]{2,1,0:T(8,128)S(1)} %copy-done.4, f32[256,1024]{1,0:T(8,128)} %copy.14, f32[1024]{0:T(1024)S(1)} %copy-done.6), kind=kLoop, calls=%fused_computation.22 | loop fusion | flops 1310720 | bytes 4722688 | tf_op jit(solution)/shard_map/convert_element_type | solution.py:269
  (5 shorter events, 0.1 us)
Async XLA Ops:
  6.5 10.4 %copy-start.5 = (f32[3,7,1024]{2,1,0:T(8,128)S(1)}, f32[3,7,1024]{2,1,0:T(8,128)}, u32[]{:S(2)}) copy-start(f32[3,7,1024]{2,1,0:T(8,128)} %param.10) | copy-start | bytes 258052
  6.5 39.6 %all-gather.2.cloned.1.call-start = ((), (), s32[]{:S(2)}) async-start(), calls=%async_computation.3 | async-start | bytes 5242880 | tf_op jit(solution)/shard_map/all_gather | solution.py:251
  9.7 73.1 %all-to-all-start.1 = ((bf16[8,256,128]{2,1,0:T(8,128)(2,1)}), bf16[8,256,128]{2,1,0:T(8,128)(2,1)S(1)}, u32[]{:S(2)}, u32[]{:S(2)}) async-start(bf16[8,256,128]{2,1,0:T(8,128)(2,1)} %bitcast.6), calls=%async_computation.1 | async-start | bytes 1048576 | tf_op jit(solution)/shard_map/all_to_all | solution.py:239
  68.0 5.1 %collective-permute-start = (bf16[3,6,1024]{2,1,0:T(8,128)(2,1)S(1)}, bf16[3,6,1024]{2,1,0:T(8,128)(2,1)S(1)}, u32[]{:S(2)}, u32[]{:S(2)}) collective-permute-start(bf16[3,6,1024]{2,1,0:T(8,128)(2,1)S(1)} %slice.68), channel_id=1, source_target_pairs={{0,4},{4,8},{8,12},{12,16},{16,20},{20,24},{24,28},{1,5},{5,9},{9,... | collective-permute-start | bytes 110600 | tf_op jit(solution)/shard_map/ppermute | solution.py:22
  76.0 1.7 %copy-start.3 = (f32[3,256,1024]{2,1,0:T(8,128)}, f32[3,256,1024]{2,1,0:T(8,128)S(1)}, u32[]{:S(2)}) copy-start(f32[3,256,1024]{2,1,0:T(8,128)S(1)} %multiply_add_fusion) | copy-start | bytes 9437188
  77.6 25.3 %copy-start = (f32[9,2,256,128]{3,2,1,0:T(8,128)S(1)}, f32[9,2,256,128]{3,2,1,0:T(8,128)}, u32[]{:S(2)}) copy-start(f32[9,2,256,128]{3,2,1,0:T(8,128)} %constant.8.clone.twist) | copy-start | bytes 7077892
  77.6 25.3 %copy-start.1 = (bf16[512,512]{1,0:T(8,128)(2,1)S(1)}, bf16[512,512]{1,0:T(8,128)(2,1)}, u32[]{:S(2)}) copy-start(bf16[512,512]{1,0:T(8,128)(2,1)} %constant.7.clone.back) | copy-start | bytes 1572868
  102.9 1.0 copy-start.2
  125.1 6.5 %copy-start.4 = (f32[3,256,1024]{2,1,0:T(8,128)S(1)}, f32[3,256,1024]{2,1,0:T(8,128)}, u32[]{:S(2)}) copy-start(f32[3,256,1024]{2,1,0:T(8,128)} %copy-done.3) | copy-start | bytes 9437188
  125.1 6.5 %copy-start.6 = (f32[1024]{0:T(1024)S(1)}, f32[1024]{0:T(1024)}, u32[]{:S(2)}) copy-start(f32[1024]{0:T(1024)} %param.12) | copy-start | bytes 12292
Sparse Core Ops, SparseCore 0:
  8.9 37.1 all-gather.1

commit v2 on v1

--- a/solution.py
+++ b/solution.py
@@ -159,31 +159,20 @@
     return jnp.concatenate([real * cos + imag * sin, imag * cos - real * sin], 0).astype(jnp.bfloat16)
 
 
-def local_convolution(blocks, rows, load_signal, load_filter, there, back, twist):
+def local_convolution(blocks, rows, load_signal, fil_real, fil_imag, there, back, twist):
     half = blocks // 2
-    signal, filt = fold(load_signal, blocks), fold(load_filter, blocks)
+    signal = fold(load_signal, blocks)
     cos_even, sin_even = [None] * (half + 1), [None] * (half + 1)
     cos_odd, sin_odd = [None] * (half + 1), [None] * (half + 1)
     plus = lambda old, new: new if old is None else (old if new is None else old + new)
     for freq in range(blocks + 1):
         cos, sin = twist[freq, 0], twist[freq, 1]
-        stacked = jnp.concatenate(
-            [
-                twisted_stage(signal, freq, blocks, cos, sin),
-                twisted_stage(filt, freq, blocks, cos, sin),
-            ],
-            1,
-        )
+        stacked = twisted_stage(signal, freq, blocks, cos, sin)
         spectrum = jnp.dot(there[...], stacked, preferred_element_type=jnp.float32)
-        sig_real, sig_imag = spectrum[:rows, :LANES], spectrum[rows:, :LANES]
-        fil_real, fil_imag = spectrum[:rows, LANES:], spectrum[rows:, LANES:]
-        scale = (1.0 if freq in (0, blocks) else 2.0) / (2 * blocks * rows)
+        sig_real, sig_imag = spectrum[:rows], spectrum[rows:]
+        by_real, by_imag = fil_real[freq], fil_imag[freq]
         product = jnp.concatenate(
-            [
-                (sig_real * fil_real - sig_imag * fil_imag) * scale,
-                (sig_real * fil_imag + sig_imag * fil_real) * scale,
-            ],
-            0,
+            [sig_real * by_real - sig_imag * by_imag, sig_real * by_imag + sig_imag * by_real], 0
         ).astype(jnp.bfloat16)
         values = jnp.dot(back[...], product, preferred_element_type=jnp.float32)
         real, imag = values[:rows], values[rows:]
@@ -202,50 +191,280 @@
     return result
 
 
-def convolution_kernel(blocks, rows, signal, filt, there, back, twist, out):
+def whole_kernel(
+    blocks, tokens, weight, taps, long_filter, skip, there, back, twist, out,
+    held, slots, acc, rim_out, rim_in, query, gated,
+    fil_out, fil_in, sig_out, sig_in, res_out, res_in, fil_real, fil_imag,
+    weight_sem, token_send, token_recv, rim_send, rim_recv,
+    fil_send, fil_recv, sig_send, sig_recv, res_send, res_recv,
+):
+    me, ch = lax.axis_index("seq"), lax.axis_index("ch")
+    rows, width = tokens.shape
+    pieces = held.shape[1]
+    part = width // pieces
+    wide = 2 * LANES
+    chunks = blocks // 2
+    level, side = me // 2, me % 2
+    mate = ch + 1 - 2 * (ch % 2)
+    across = (ch + 2) % 4
+    across_mate = (mate + 2) % 4
+    mesh_id = pl.DeviceIdType.MESH
+
+    order = [(ch, None, q) for q in range(pieces)] + [(mate, 0, q) for q in range(pieces)]
+    for q in range(pieces):
+        order += [(across, 1, q), (across_mate, 2, q)]
+    slot_count = slots.shape[0]
+
+    def weight_copy(k):
+        shard, _, q = order[k]
+        first = pl.multiple_of(shard * width + q * part, part)
+        return pltpu.make_async_copy(
+            weight.at[:, pl.ds(first, part), :], slots.at[k % slot_count], weight_sem.at[k % slot_count]
+        )
+
+    def remote(src, dst, send, recv, **where):
+        return pltpu.make_async_remote_copy(
+            src_ref=src, dst_ref=dst, send_sem=send, recv_sem=recv, device_id=where, device_id_type=mesh_id
+        )
+
+    for k in range(slot_count):
+        weight_copy(k).start()
+
+    barrier = pltpu.get_barrier_semaphore()
+    for far in range(1, blocks):
+        pl.semaphore_signal(barrier, inc=1, device_id={"seq": (me + far) % blocks}, device_id_type=mesh_id)
+    pl.semaphore_signal(barrier, inc=1, device_id={"ch": mate}, device_id_type=mesh_id)
+    pl.semaphore_signal(barrier, inc=1, device_id={"ch": across}, device_id_type=mesh_id)
+    for d in range(blocks):
+        fil_out[d] = long_filter[:, d * LANES : (d + 1) * LANES].astype(jnp.bfloat16)
+    pl.semaphore_wait(barrier, blocks + 1)
+
+    own_piece = lambda q: tokens.at[:, q * part : (q + 1) * part]
+    to_across = [
+        remote(own_piece(q), held.at[1, q], token_send.at[1, q], token_recv.at[1, q], ch=across)
+        for q in range(pieces)
+    ]
+    to_mate = [
+        remote(own_piece(q), held.at[0, q], token_send.at[0, q], token_recv.at[0, q], ch=mate)
+        for q in range(pieces)
+    ]
+    hand_on = [
+        remote(held.at[1, q], held.at[2, q], token_send.at[2, q], token_recv.at[2, q], ch=mate)
+        for q in range(pieces)
+    ]
+
+    def to_block(out_buf, in_buf, send, recv, d):
+        return remote(out_buf.at[d], in_buf.at[me], send.at[d], recv.at[me], seq=d)
+
+    def from_block(out_buf, in_buf, send, recv, d):
+        return remote(out_buf.at[d], in_buf.at[d], send.at[d], recv.at[d], seq=d)
+
+    fil = (fil_out, fil_in, fil_send, fil_recv)
+    sig = (sig_out, sig_in, sig_send, sig_recv)
+    res = (res_out, res_in, res_send, res_recv)
+    for q in range(pieces):
+        to_across[q].start()
+        to_mate[q].start()
+    for far in range(1, blocks):
+        to_block(*fil, (me + far) % blocks).start()
+    fil_in[me] = fil_out[me]
+
+    def piece(k):
+        _, place, q = order[k]
+        return tokens[:, q * part : (q + 1) * part] if place is None else held[place, q]
+
+    def product(k, chunk, j):
+        columns = pl.ds(pl.multiple_of(chunk * wide, wide), wide)
+        total = None
+        for kk in (k, k + 1):
+            term = jnp.dot(piece(kk), slots[kk % slot_count, j, :, columns], preferred_element_type=jnp.float32)
+            total = term if total is None else total + term
+        return total
+
+    def arrive(k):
+        for kk in (k, k + 1):
+            _, place, q = order[kk]
+            if place is not None:
+                (to_mate, to_across, hand_on)[place][q].wait_recv()
+            if place == 1:
+                hand_on[q].start()
+        for kk in (k, k + 1):
+            weight_copy(kk).wait()
+
+    def filter_spectrum():
+        for far in range(1, blocks):
+            from_block(*fil, (me + far) % blocks).wait_recv()
+        folded = fold(lambda j: fil_in[j].astype(jnp.float32), blocks)
+        for freq in range(blocks + 1):
+            stacked = twisted_stage(folded, freq, blocks, twist[freq, 0], twist[freq, 1])
+            spectrum = jnp.dot(there[...], stacked, preferred_element_type=jnp.float32)
+            scale = (1.0 if freq in (0, blocks) else 2.0) / (2 * blocks * rows)
+            fil_real[freq] = spectrum[:rows] * scale
+            fil_imag[freq] = spectrum[rows:] * scale
+
+    total_tiles = len(order)
+    for k in range(0, total_tiles - 2, 2):
+        arrive(k)
+
+        def accumulate(n, carry, k=k):
+            chunk, j = n // 3, n % 3
+            value = product(k, chunk, j)
+            if k == 0:
+                acc[chunk, j, 8:, :] = value
+            else:
+                acc[chunk, j, 8:, :] += value
+            return carry
+
+        lax.fori_loop(0, 3 * chunks, accumulate, 0)
+        for kk in (k, k + 1):
+            if kk + slot_count < total_tiles:
+                weight_copy(kk + slot_count).start()
+        if k + 2 == 2 * pieces:
+            filter_spectrum()
+    last = total_tiles - 2
+    arrive(last)
+
+    chunk_of = lambda s: (level - s + chunks) % chunks
+    following = (me + 1) % blocks
+
+    def rim_copy(chunk):
+        return remote(rim_out.at[chunk], rim_in.at[chunk], rim_send.at[chunk], rim_recv.at[chunk], seq=following)
+
+    def project(s):
+        chunk = chunk_of(s)
+
+        def one(j, carry):
+            value = (acc[chunk, j, 8:, :] + product(last, chunk, j)).astype(jnp.bfloat16)
+            acc[chunk, j, 8:, :] = value.astype(jnp.float32)
+            rim_out[chunk, j] = value[rows - 16 :]
+            return carry
+
+        lax.fori_loop(0, 3, one, 0)
+        rim_copy(chunk).start()
+
+    def short_filter(s):
+        chunk = chunk_of(s)
+        rim_copy(chunk).wait_recv()
+        columns = pl.ds(pl.multiple_of(chunk * wide, wide), wide)
+        results = []
+        for j in range(3):
+            rim = rim_in[chunk, j][8:].astype(jnp.float32)
+            acc[chunk, j, :8, :] = jnp.where(me > 0, rim, 0.0)
+            total = None
+            for i in range(TAPS):
+                term = taps[j, i : i + 1, columns] * acc[chunk, j, 8 - i : 8 - i + rows, :]
+                total = term if total is None else total + term
+            results.append(total)
+        inputs = results[1] * results[2]
+        for half in range(2):
+            d = 2 * chunk + half
+            lanes = slice(half * LANES, (half + 1) * LANES)
+            query[d] = results[0][:, lanes]
+            gated[d] = inputs[:, lanes]
+            sig_out[d] = inputs[:, lanes].astype(jnp.bfloat16)
+        if s == 0:
+            to_block(*sig, 2 * level + 1 - side).start()
+            sig_in[me] = sig_out[me]
+        else:
+            to_block(*sig, 2 * chunk).start()
+            to_block(*sig, 2 * chunk + 1).start()
+
+    for s in range(chunks):
+        project(s)
+        if s >= 2:
+            short_filter(s - 1)
+    short_filter(chunks - 1)
+    short_filter(0)
+
+    for far in range(1, blocks):
+        from_block(*sig, (me + far) % blocks).wait_recv()
     result = local_convolution(
-        blocks,
-        rows,
-        lambda j: signal[j].astype(jnp.float32),
-        lambda j: filt[j].astype(jnp.float32),
-        there,
-        back,
-        twist,
+        blocks, rows, lambda j: sig_in[j].astype(jnp.float32), fil_real, fil_imag, there, back, twist
     )
     for j in range(blocks):
-        out[j] = result[j].astype(out.dtype)
-
-
-def narrow_convolution(signal, spread_filter):
+        res_out[j] = result[j].astype(jnp.bfloat16)
+    for far in range(1, blocks):
+        to_block(*res, (me + far) % blocks).start()
+    res_in[me] = res_out[me]
+
+    def finish(far, carry):
+        d = (me + far) % blocks
+        columns = pl.ds(pl.multiple_of(d * LANES, LANES), LANES)
+        conv = res_in[d].astype(jnp.float32)
+        out[:, columns] = (query[d] * (conv + skip[:, columns] * gated[d])).astype(jnp.bfloat16)
+        return carry
+
+    for far in range(blocks):
+        if far:
+            from_block(*res, (me + far) % blocks).wait_recv()
+        finish(far, 0)
+
+    for q in range(pieces):
+        to_across[q].wait_send()
+        to_mate[q].wait_send()
+        hand_on[q].wait_send()
+    for far in range(1, blocks):
+        d = (me + far) % blocks
+        to_block(*fil, d).wait_send()
+        to_block(*sig, d).wait_send()
+        to_block(*res, d).wait_send()
+    for s in range(chunks):
+        rim_copy(chunk_of(s)).wait_send()
+
+
+def whole_operator(tokens, proj_weight, short_taps, long_filter, skip_gain):
     blocks = lax.axis_size("seq")
-    rows = signal.shape[0]
-    spread_signal = exchange(signal)
-    there, back, twist = transform_tables(blocks, rows)
-    out = pl.pallas_call(
-        functools.partial(convolution_kernel, blocks, rows),
-        out_shape=jax.ShapeDtypeStruct((blocks, rows, LANES), jnp.bfloat16),
-        in_specs=[pl.BlockSpec(memory_space=pltpu.VMEM)] * 5,
-        out_specs=pl.BlockSpec(memory_space=pltpu.VMEM),
-        compiler_params=pltpu.CompilerParams(vmem_limit_bytes=48 * 1024 * 1024),
-        name="long_convolution",
-    )(spread_signal, spread_filter, there, back, twist)
-    gathered = lax.all_to_all(out, "seq", split_axis=0, concat_axis=0, tiled=True)
-    return jnp.swapaxes(gathered, 0, 1).reshape(signal.shape).astype(jnp.float32)
-
-
-def exchange(values):
-    blocks = lax.axis_size("seq")
-    parts = values.astype(jnp.bfloat16).reshape(values.shape[0], blocks, LANES)
-    return lax.all_to_all(jnp.swapaxes(parts, 0, 1), "seq", split_axis=0, concat_axis=0, tiled=True)
+    rows, width = tokens.shape
+    channels = proj_weight.shape[2]
+    pieces = 4
+    part = width // pieces
+    chunks = blocks // 2
+    lane_blocks = pltpu.VMEM((blocks, rows, LANES), jnp.bfloat16)
+    lane_blocks_f32 = pltpu.VMEM((blocks, rows, LANES), jnp.float32)
+    spectrum = pltpu.VMEM((blocks + 1, rows, LANES), jnp.float32)
+    vmem = pl.BlockSpec(memory_space=pltpu.VMEM)
+    slot_count = 8
+    return pl.pallas_call(
+        functools.partial(whole_kernel, blocks),
+        out_shape=jax.ShapeDtypeStruct((rows, channels), jnp.bfloat16),
+        in_specs=[vmem, pl.BlockSpec(memory_space=pl.ANY)] + [vmem] * 6,
+        out_specs=vmem,
+        scratch_shapes=[
+            pltpu.VMEM((3, pieces, rows, part), jnp.bfloat16),
+            pltpu.VMEM((slot_count, 3, part, channels), jnp.bfloat16),
+            pltpu.VMEM((chunks, 3, rows + 8, 2 * LANES), jnp.float32),
+            pltpu.VMEM((chunks, 3, 16, 2 * LANES), jnp.bfloat16),
+            pltpu.VMEM((chunks, 3, 16, 2 * LANES), jnp.bfloat16),
+            lane_blocks_f32,
+            lane_blocks_f32,
+        ]
+        + [lane_blocks] * 6
+        + [spectrum] * 2
+        + [pltpu.SemaphoreType.DMA((slot_count,))]
+        + [pltpu.SemaphoreType.DMA((3, pieces))] * 2
+        + [pltpu.SemaphoreType.DMA((chunks,))] * 2
+        + [pltpu.SemaphoreType.DMA((blocks,))] * 6,
+        compiler_params=pltpu.CompilerParams(
+            collective_id=0, has_side_effects=True, vmem_limit_bytes=58 * 1024 * 1024
+        ),
+        name="hyena_operator",
+    )(
+        tokens,
+        proj_weight,
+        short_taps,
+        long_filter,
+        skip_gain.reshape(1, channels),
+        *transform_tables(blocks, rows),
+    )
 
 
 def per_device(tokens, proj_weight, short_taps, long_filter, skip_gain):
     row_count = tokens.shape[0]
     chan_count = proj_weight.shape[2]
     seq_count = lax.axis_size("seq")
-    narrow = chan_count == seq_count * LANES and row_count % 16 == 0 and seq_count % 4 == 0
-    if narrow:
-        spread_filter = exchange(long_filter)
+    lane_tiles = chan_count == seq_count * LANES and seq_count % 4 == 0
+    if lane_tiles and row_count % 16 == 0 and lax.axis_size("ch") == 4 and tokens.shape[1] % 512 == 0:
+        return whole_operator(tokens, proj_weight, short_taps, long_filter, skip_gain)
     projected = jnp.einsum(
         "td,jdc->jtc",
         lax.all_gather(tokens, "ch", axis=1, tiled=True),
@@ -262,10 +481,7 @@
         ].astype(jnp.float32)
     query_part = filtered[0]
     gated_input = filtered[1] * filtered[2]
-    if narrow:
-        long_conv = narrow_convolution(gated_input, spread_filter)
-    else:
-        long_conv = spread_convolution(gated_input, long_filter)
+    long_conv = spread_convolution(gated_input, long_filter)
     return (query_part * (long_conv + skip_gain * gated_input)).astype(jnp.bfloat16)
 
 

time: 141 us -> 77.9 us (0.55)
  Pallas kernels: 3.76 us -> 74.9 us
  blocking collectives: 37.6 us -> 0 us
  waiting for transfers between devices: 31.5 us -> 0 us
  matrix products: 21.8 us -> 0 us
  between operations: 13.5 us -> 0.01 us
  local copies, waits for them, and re-layouts: 14.9 us -> 1.87 us
  starting transfers between devices: 10.6 us -> 0 us
  other arithmetic: 7.3 us -> 0 us
    pallas_call x1, Pallas kernels: 3.76 us -> 74.9 us  [whole_operator(): pl.pallas_call(functools.partial(whole_kernel, blocks), out_shape=jax.Sha...]
    all_to_all x2 -> x0, blocking collectives: 37.6 us -> none  [the longest x1 20.1 us: exchange(): lax.all_to_all(jnp.swapaxes(parts, 0, 1), 'seq', split_axis=0, concat_axi...]
    all_gather x1 -> x0, waiting for transfers between devices: 29.1 us -> none  [per_device(): lax.all_gather(tokens, 'ch', axis=1, tiled=True)]
    dot_general x1 -> x0, matrix products: 21.8 us -> none  [per_device(): jnp.einsum('td,jdc->jtc', lax.all_gather(tokens, 'ch', axis=1, tiled=True...]
    convert_element_type x4 -> x0, local copies, waits for them, and re-layouts: 9.6 us -> none  [the longest x2 5.4 us: narrow_convolution(): jnp.swapaxes(gathered, 0, 1).reshape(signal.shape).astype(jnp.float32)]
    all_to_all x1 -> x0, starting transfers between devices: 7.25 us -> none  [exchange(): lax.all_to_all(jnp.swapaxes(parts, 0, 1), 'seq', split_axis=0, concat_axi...]
    convert_element_type x3 -> x0, other arithmetic: 4.43 us -> none  [the longest x1 2.45 us: per_device(): (query_part * (long_conv + skip_gain * gated_input)).astype(jnp.bfloat16)]
    ppermute x1 -> x0, starting transfers between devices: 3.37 us -> none  [shifted(): return lax.ppermute(value, axis, pairs)]
  transfers between devices with their start and end apart: 3 -> 0, of which waited for: 2 -> 0; matrix products, arithmetic and copies ran while one was open for 23% -> 0% of each run, Pallas kernels for 0% -> 0%
where the time goes in v2:
time: 77.9 us; the launch traced here: 76.7 us
  Pallas kernels  74.9 us (96%)
  local copies, waits for them, and re-layouts  1.87 us (2%)
    pallas_call x1, Pallas kernels, whole_operator(): pl.pallas_call(functools.partial(whole_kernel, blocks), out_shape=jax.Sha...  74.9 us
    unnamed x1, local copies, waits for them, and re-layouts  1.87 us

profile of v2, /device:TPU:0, one launch (start us, length us, event | category | flops | bytes accessed | tf_op | source)
XLA Modules:
  0.0 76.7 jit_solution(5709913167475760280)
XLA Ops:
  0.0 74.9 %hyena_operator.1 = bf16[256,1024]{1,0:T(8,128)(2,1)} custom-call(bf16[256,2048]{1,0:T(8,128)(2,1)} %tokens.1, bf16[3,8192,1024]{2,1,0:T(8,128)(2,1)} %weight.1, f32[3,7,1024]{2,1,0:T(8,128)} %taps.1, f32[256,1024]{1,0:T(8,128)} %long_filter.1, f32[1,1024]{1,0:T(1,128)} %bitcast.1, bf16[512,512]{1,0:T(8,128)(2,1)} %constant.6.clone.there, ...), custom_call_target="tpu_custom_call" | custom-call | tf_op jit(solution)/shard_map/hyena_operator/pallas_call | solution.py:427
  74.9 1.9 %copy.10 = bf16[256,1024]{1,0:T(8,128)(2,1)} copy(bf16[256,1024]{1,0:T(8,128)(2,1)} %hyena_operator.1) | data formatting | bytes 1048576

commit v3 on v2

--- a/solution.py
+++ b/solution.py
@@ -192,10 +192,11 @@
 
 
 def whole_kernel(
-    blocks, tokens, weight, taps, long_filter, skip, there, back, twist, out,
+    blocks, tokens, weight, taps, filter_hbm, skip, there_hbm, back_hbm, twist_hbm, out,
+    long_filter, there, back, twist, own,
     held, slots, acc, rim_out, rim_in, query, gated,
     fil_out, fil_in, sig_out, sig_in, res_out, res_in, fil_real, fil_imag,
-    weight_sem, token_send, token_recv, rim_send, rim_recv,
+    input_sem, own_sem, weight_sem, token_send, token_recv, rim_send, rim_recv,
     fil_send, fil_recv, sig_send, sig_recv, res_send, res_recv,
 ):
     me, ch = lax.axis_index("seq"), lax.axis_index("ch")
@@ -209,6 +210,7 @@
     across = (ch + 2) % 4
     across_mate = (mate + 2) % 4
     mesh_id = pl.DeviceIdType.MESH
+    farthest_first = sorted(range(1, blocks), key=lambda far: abs(far - blocks // 2))
 
     order = [(ch, None, q) for q in range(pieces)] + [(mate, 0, q) for q in range(pieces)]
     for q in range(pieces):
@@ -227,7 +229,22 @@
             src_ref=src, dst_ref=dst, send_sem=send, recv_sem=recv, device_id=where, device_id_type=mesh_id
         )
 
-    for k in range(slot_count):
+    filter_copy = pltpu.make_async_copy(filter_hbm, long_filter, input_sem.at[0])
+    table_copies = [
+        pltpu.make_async_copy(there_hbm, there, input_sem.at[1]),
+        pltpu.make_async_copy(back_hbm, back, input_sem.at[2]),
+        pltpu.make_async_copy(twist_hbm, twist, input_sem.at[3]),
+    ]
+    own_piece = lambda q: tokens.at[:, q * part : (q + 1) * part]
+    own_copies = [pltpu.make_async_copy(own_piece(q), own.at[q], own_sem.at[q]) for q in range(pieces)]
+    filter_copy.start()
+    own_copies[0].start()
+    own_copies[1].start()
+    weight_copy(0).start()
+    weight_copy(1).start()
+    own_copies[2].start()
+    own_copies[3].start()
+    for k in range(2, slot_count):
         weight_copy(k).start()
 
     barrier = pltpu.get_barrier_semaphore()
@@ -235,11 +252,11 @@
         pl.semaphore_signal(barrier, inc=1, device_id={"seq": (me + far) % blocks}, device_id_type=mesh_id)
     pl.semaphore_signal(barrier, inc=1, device_id={"ch": mate}, device_id_type=mesh_id)
     pl.semaphore_signal(barrier, inc=1, device_id={"ch": across}, device_id_type=mesh_id)
+    filter_copy.wait()
     for d in range(blocks):
         fil_out[d] = long_filter[:, d * LANES : (d + 1) * LANES].astype(jnp.bfloat16)
     pl.semaphore_wait(barrier, blocks + 1)
 
-    own_piece = lambda q: tokens.at[:, q * part : (q + 1) * part]
     to_across = [
         remote(own_piece(q), held.at[1, q], token_send.at[1, q], token_recv.at[1, q], ch=across)
         for q in range(pieces)
@@ -262,16 +279,17 @@
     fil = (fil_out, fil_in, fil_send, fil_recv)
     sig = (sig_out, sig_in, sig_send, sig_recv)
     res = (res_out, res_in, res_send, res_recv)
+    to_across[0].start()
     for q in range(pieces):
-        to_across[q].start()
         to_mate[q].start()
-    for far in range(1, blocks):
+    to_across[1].start()
+    for far in farthest_first:
         to_block(*fil, (me + far) % blocks).start()
     fil_in[me] = fil_out[me]
 
     def piece(k):
         _, place, q = order[k]
-        return tokens[:, q * part : (q + 1) * part] if place is None else held[place, q]
+        return own[q] if place is None else held[place, q]
 
     def product(k, chunk, j):
         columns = pl.ds(pl.multiple_of(chunk * wide, wide), wide)
@@ -284,14 +302,20 @@
     def arrive(k):
         for kk in (k, k + 1):
             _, place, q = order[kk]
-            if place is not None:
+            if place is None:
+                own_copies[q].wait()
+            else:
                 (to_mate, to_across, hand_on)[place][q].wait_recv()
             if place == 1:
                 hand_on[q].start()
+                if q + 2 < pieces:
+                    to_across[q + 2].start()
         for kk in (k, k + 1):
             weight_copy(kk).wait()
 
     def filter_spectrum():
+        for copy in table_copies:
+            copy.wait()
         for far in range(1, blocks):
             from_block(*fil, (me + far) % blocks).wait_recv()
         folded = fold(lambda j: fil_in[j].astype(jnp.float32), blocks)
@@ -319,8 +343,9 @@
         for kk in (k, k + 1):
             if kk + slot_count < total_tiles:
                 weight_copy(kk + slot_count).start()
-        if k + 2 == 2 * pieces:
-            filter_spectrum()
+        if k == slot_count:
+            for copy in table_copies:
+                copy.start()
     last = total_tiles - 2
     arrive(last)
 
@@ -375,6 +400,7 @@
             short_filter(s - 1)
     short_filter(chunks - 1)
     short_filter(0)
+    filter_spectrum()
 
     for far in range(1, blocks):
         from_block(*sig, (me + far) % blocks).wait_recv()
@@ -383,7 +409,7 @@
     )
     for j in range(blocks):
         res_out[j] = result[j].astype(jnp.bfloat16)
-    for far in range(1, blocks):
+    for far in farthest_first:
         to_block(*res, (me + far) % blocks).start()
     res_in[me] = res_out[me]
 
@@ -423,13 +449,18 @@
     lane_blocks_f32 = pltpu.VMEM((blocks, rows, LANES), jnp.float32)
     spectrum = pltpu.VMEM((blocks + 1, rows, LANES), jnp.float32)
     vmem = pl.BlockSpec(memory_space=pltpu.VMEM)
+    hbm = pl.BlockSpec(memory_space=pl.ANY)
     slot_count = 8
+    tables = transform_tables(blocks, rows)
     return pl.pallas_call(
         functools.partial(whole_kernel, blocks),
         out_shape=jax.ShapeDtypeStruct((rows, channels), jnp.bfloat16),
-        in_specs=[vmem, pl.BlockSpec(memory_space=pl.ANY)] + [vmem] * 6,
+        in_specs=[hbm, hbm, vmem, hbm, vmem, hbm, hbm, hbm],
         out_specs=vmem,
-        scratch_shapes=[
+        scratch_shapes=[pltpu.VMEM(long_filter.shape, jnp.float32)]
+        + [pltpu.VMEM(table.shape, table.dtype) for table in tables]
+        + [
+            pltpu.VMEM((pieces, rows, part), jnp.bfloat16),
             pltpu.VMEM((3, pieces, rows, part), jnp.bfloat16),
             pltpu.VMEM((slot_count, 3, part, channels), jnp.bfloat16),
             pltpu.VMEM((chunks, 3, rows + 8, 2 * LANES), jnp.float32),
@@ -440,6 +471,7 @@
         ]
         + [lane_blocks] * 6
         + [spectrum] * 2
+        + [pltpu.SemaphoreType.DMA((4,)), pltpu.SemaphoreType.DMA((pieces,))]
         + [pltpu.SemaphoreType.DMA((slot_count,))]
         + [pltpu.SemaphoreType.DMA((3, pieces))] * 2
         + [pltpu.SemaphoreType.DMA((chunks,))] * 2
@@ -454,7 +486,7 @@
         short_taps,
         long_filter,
         skip_gain.reshape(1, channels),
-        *transform_tables(blocks, rows),
+        *tables,
     )
 
 

time: 77.9 us -> 79.9 us (1.026); the launches traced: 76.7 us -> 79.8 us
  Pallas kernels: 74.9 us -> 77.9 us
    pallas_call x1, Pallas kernels: 74.9 us -> 77.9 us  [whole_operator(): pl.pallas_call(functools.partial(whole_kernel, blocks), out_shape=jax.Sha...]
where the time goes in v3:
time: 79.9 us; the launch traced here: 79.8 us
  Pallas kernels  77.9 us (97%)
  local copies, waits for them, and re-layouts  1.87 us (2%)
    pallas_call x1, Pallas kernels, whole_operator(): pl.pallas_call(functools.partial(whole_kernel, blocks), out_shape=jax.Sha...  77.9 us
    unnamed x1, local copies, waits for them, and re-layouts  1.87 us

profile of v3, /device:TPU:0, one launch (start us, length us, event | category | flops | bytes accessed | tf_op | source)
XLA Modules:
  0.0 79.8 jit_solution(8136930562842142714)
XLA Ops:
  0.0 77.9 %hyena_operator.1 = bf16[256,1024]{1,0:T(8,128)(2,1)} custom-call(bf16[256,2048]{1,0:T(8,128)(2,1)} %tokens.1, bf16[3,8192,1024]{2,1,0:T(8,128)(2,1)} %weight.1, f32[3,7,1024]{2,1,0:T(8,128)} %taps.1, f32[256,1024]{1,0:T(8,128)} %filter_hbm.1, f32[1,1024]{1,0:T(1,128)} %bitcast.1, bf16[512,512]{1,0:T(8,128)(2,1)} %constant.6.clone.there_hbm, ...), custom_call_target="tpu_custom_call" | custom-call | tf_op jit(solution)/shard_map/hyena_operator/pallas_call | solution.py:455
  77.9 1.9 %copy.10 = bf16[256,1024]{1,0:T(8,128)(2,1)} copy(bf16[256,1024]{1,0:T(8,128)(2,1)} %hyena_operator.1) | data formatting | bytes 1048576

commit v4 on v3

--- a/solution.py
+++ b/solution.py
@@ -216,6 +216,8 @@
     for q in range(pieces):
         order += [(across, 1, q), (across_mate, 2, q)]
     slot_count = slots.shape[0]
+    group = pieces
+    strip_rows = 32
 
     def weight_copy(k):
         shard, _, q = order[k]
@@ -294,13 +296,13 @@
     def product(k, chunk, j):
         columns = pl.ds(pl.multiple_of(chunk * wide, wide), wide)
         total = None
-        for kk in (k, k + 1):
+        for kk in range(k, k + group):
             term = jnp.dot(piece(kk), slots[kk % slot_count, j, :, columns], preferred_element_type=jnp.float32)
             total = term if total is None else total + term
         return total
 
     def arrive(k):
-        for kk in (k, k + 1):
+        for kk in range(k, k + group):
             _, place, q = order[kk]
             if place is None:
                 own_copies[q].wait()
@@ -310,7 +312,7 @@
                 hand_on[q].start()
                 if q + 2 < pieces:
                     to_across[q + 2].start()
-        for kk in (k, k + 1):
+        for kk in range(k, k + group):
             weight_copy(kk).wait()
 
     def filter_spectrum():
@@ -327,26 +329,26 @@
             fil_imag[freq] = spectrum[rows:] * scale
 
     total_tiles = len(order)
-    for k in range(0, total_tiles - 2, 2):
+    for k in range(0, total_tiles - group, group):
         arrive(k)
 
-        def accumulate(n, carry, k=k):
-            chunk, j = n // 3, n % 3
-            value = product(k, chunk, j)
-            if k == 0:
-                acc[chunk, j, 8:, :] = value
-            else:
-                acc[chunk, j, 8:, :] += value
+        def accumulate(chunk, carry, k=k):
+            for j in range(3):
+                value = product(k, chunk, j)
+                if k == 0:
+                    acc[chunk, j, 8:, :] = value
+                else:
+                    acc[chunk, j, 8:, :] += value
             return carry
 
-        lax.fori_loop(0, 3 * chunks, accumulate, 0)
-        for kk in (k, k + 1):
+        lax.fori_loop(0, chunks, accumulate, 0)
+        for kk in range(k, k + group):
             if kk + slot_count < total_tiles:
                 weight_copy(kk + slot_count).start()
-        if k == slot_count:
+        if k == group:
             for copy in table_copies:
                 copy.start()
-    last = total_tiles - 2
+    last = total_tiles - group
     arrive(last)
 
     chunk_of = lambda s: (level - s + chunks) % chunks
@@ -358,48 +360,63 @@
     def project(s):
         chunk = chunk_of(s)
 
-        def one(j, carry):
+        for j in range(3):
             value = (acc[chunk, j, 8:, :] + product(last, chunk, j)).astype(jnp.bfloat16)
             acc[chunk, j, 8:, :] = value.astype(jnp.float32)
             rim_out[chunk, j] = value[rows - 16 :]
-            return carry
-
-        lax.fori_loop(0, 3, one, 0)
         rim_copy(chunk).start()
 
-    def short_filter(s):
+    def short_filter(s, first=False):
         chunk = chunk_of(s)
         rim_copy(chunk).wait_recv()
         columns = pl.ds(pl.multiple_of(chunk * wide, wide), wide)
-        results = []
         for j in range(3):
             rim = rim_in[chunk, j][8:].astype(jnp.float32)
             acc[chunk, j, :8, :] = jnp.where(me > 0, rim, 0.0)
-            total = None
-            for i in range(TAPS):
-                term = taps[j, i : i + 1, columns] * acc[chunk, j, 8 - i : 8 - i + rows, :]
-                total = term if total is None else total + term
-            results.append(total)
-        inputs = results[1] * results[2]
-        for half in range(2):
-            d = 2 * chunk + half
-            lanes = slice(half * LANES, (half + 1) * LANES)
-            query[d] = results[0][:, lanes]
-            gated[d] = inputs[:, lanes]
-            sig_out[d] = inputs[:, lanes].astype(jnp.bfloat16)
-        if s == 0:
+
+        def strip(r, carry):
+            begin = pl.multiple_of(r * strip_rows, strip_rows)
+            results = []
+            for j in range(3):
+                window = acc[chunk, j, pl.ds(begin, strip_rows + 8), :]
+                total = None
+                for i in range(TAPS):
+                    term = taps[j, i : i + 1, columns] * window[8 - i : 8 - i + strip_rows]
+                    total = term if total is None else total + term
+                results.append(total)
+            inputs = results[1] * results[2]
+            here = pl.ds(begin, strip_rows)
+            for half in range(2):
+                d = 2 * chunk + half
+                lanes = slice(half * LANES, (half + 1) * LANES)
+                query[d, here, :] = results[0][:, lanes]
+                gated[d, here, :] = inputs[:, lanes]
+                sig_out[d, here, :] = inputs[:, lanes].astype(jnp.bfloat16)
+            return carry
+
+        lax.fori_loop(0, rows // strip_rows, strip, 0)
+        if first:
             to_block(*sig, 2 * level + 1 - side).start()
             sig_in[me] = sig_out[me]
         else:
             to_block(*sig, 2 * chunk).start()
             to_block(*sig, 2 * chunk + 1).start()
 
-    for s in range(chunks):
+    def steps(begin, end, act):
+        def body(s, carry):
+            act(s)
+            return carry
+
+        lax.fori_loop(begin, end, body, 0)
+
+    def both(s):
         project(s)
-        if s >= 2:
-            short_filter(s - 1)
+        short_filter(s - 1)
+
+    steps(0, 2, project)
+    steps(2, chunks, both)
     short_filter(chunks - 1)
-    short_filter(0)
+    short_filter(0, first=True)
     filter_spectrum()
 
     for far in range(1, blocks):
@@ -495,7 +512,7 @@
     chan_count = proj_weight.shape[2]
     seq_count = lax.axis_size("seq")
     lane_tiles = chan_count == seq_count * LANES and seq_count % 4 == 0
-    if lane_tiles and row_count % 16 == 0 and lax.axis_size("ch") == 4 and tokens.shape[1] % 512 == 0:
+    if lane_tiles and row_count % 32 == 0 and lax.axis_size("ch") == 4 and tokens.shape[1] % 512 == 0:
         return whole_operator(tokens, proj_weight, short_taps, long_filter, skip_gain)
     projected = jnp.einsum(
         "td,jdc->jtc",

time: 79.9 us -> 73.7 us (0.922)
  Pallas kernels: 77.9 us -> 71.7 us
    pallas_call x1, Pallas kernels: 77.9 us -> 71.7 us  [whole_operator(): pl.pallas_call(functools.partial(whole_kernel, blocks), out_shape=jax.Sha...]
where the time goes in v4:
time: 73.7 us; the launch traced here: 73.5 us
  Pallas kernels  71.7 us (97%)
  local copies, waits for them, and re-layouts  1.87 us (3%)
    pallas_call x1, Pallas kernels, whole_operator(): pl.pallas_call(functools.partial(whole_kernel, blocks), out_shape=jax.Sha...  71.7 us
    unnamed x1, local copies, waits for them, and re-layouts  1.87 us

profile of v4, /device:TPU:0, one launch (start us, length us, event | category | flops | bytes accessed | tf_op | source)
XLA Modules:
  0.0 73.5 jit_solution(6156695837961491087)
XLA Ops:
  0.0 71.7 %hyena_operator.1 = bf16[256,1024]{1,0:T(8,128)(2,1)} custom-call(bf16[256,2048]{1,0:T(8,128)(2,1)} %tokens.1, bf16[3,8192,1024]{2,1,0:T(8,128)(2,1)} %weight.1, f32[3,7,1024]{2,1,0:T(8,128)} %taps.1, f32[256,1024]{1,0:T(8,128)} %filter_hbm.1, f32[1,1024]{1,0:T(1,128)} %bitcast.1, bf16[512,512]{1,0:T(8,128)(2,1)} %constant.6.clone.there_hbm, ...), custom_call_target="tpu_custom_call" | custom-call | tf_op jit(solution)/shard_map/hyena_operator/pallas_call | solution.py:472
  71.7 1.9 %copy.10 = bf16[256,1024]{1,0:T(8,128)(2,1)} copy(bf16[256,1024]{1,0:T(8,128)(2,1)} %hyena_operator.1) | data formatting | bytes 1048576
